TPU v7x, 32 devices: a whole 2x2x4 slice. The times are simulated.
32 devices in a mesh: rep: 4 (over z), shard: 8 (over y, x, core).
Axes of the slice: x: 2, y: 2, z: 4, core: 2. Of those that a mesh axis runs over, the one named last changes fastest.
Arguments:
- tokens: bfloat16 [8192, 1024], P(('rep', 'shard')), may hold values from -6 to 6
- cotangent: bfloat16 [8192, 1024], P(('rep', 'shard')), may hold values from -6 to 6
- deal: int32 [8192], P(('rep', 'shard')), may hold values from 0 to 2047, as said below
- offsets: int32 [32, 4], P(('rep', 'shard')), may hold values from 0 to 256, as said below
- lengths: int32 [32, 4], P(('rep', 'shard')), may hold values from 0 to 256, as said below
- norm1_gain: bfloat16 [1024], P('shard'), may hold values from 0.5 to 1.5
- q_weight: bfloat16 [1024, 768], P('shard'), may hold values from -0.1875 to 0.1875
- k_weight: bfloat16 [1024, 768], P('shard'), may hold values from -0.1875 to 0.1875
- v_weight: bfloat16 [1024, 1536], P('shard'), may hold values from -0.1875 to 0.1875
- conv_weight: bfloat16 [4, 3072], P(None, 'shard'), may hold values from -3 to 3
- beta_weight: bfloat16 [1024, 6], P('shard'), may hold values from -0.1875 to 0.1875
- decay_weight: bfloat16 [1024, 6], P('shard'), may hold values from -0.1875 to 0.1875
- log_rate: float32 [6], replicated, may hold values from -6.2 to -3
- step_bias: float32 [6], replicated, may hold values from -1 to 1
- out_gate_weight: bfloat16 [1024, 1536], P('shard'), may hold values from -0.1875 to 0.1875
- out_norm_gain: bfloat16 [256], P('shard'), may hold values from 0.5 to 1.5
- out_weight: bfloat16 [1536, 1024], P('shard'), may hold values from -0.15625 to 0.15625
- norm2_gain: bfloat16 [1024], P('shard'), may hold values from 0.5 to 1.5
- ffn_gate: bfloat16 [1024, 2816], P('shard'), may hold values from -0.1875 to 0.1875
- ffn_up: bfloat16 [1024, 2816], P('shard'), may hold values from -0.1875 to 0.1875
- ffn_down: bfloat16 [2816, 1024], P('shard'), may hold values from -0.109375 to 0.109375
Outputs:
- mixed_rows: bfloat16 [8192, 1024], P(('rep', 'shard'))
- tokens_grad: bfloat16 [8192, 1024], P(('rep', 'shard'))
- norm1_gain_grad: float32 [1024], P('shard')
- q_weight_grad: float32 [1024, 768], P('shard')
- k_weight_grad: float32 [1024, 768], P('shard')
- v_weight_grad: float32 [1024, 1536], P('shard')
- conv_weight_grad: float32 [4, 3072], P(None, 'shard')
- beta_weight_grad: float32 [1024, 6], P('shard')
- decay_weight_grad: float32 [1024, 6], P('shard')
- log_rate_grad: float32 [6], replicated
- step_bias_grad: float32 [6], replicated
- out_gate_weight_grad: float32 [1024, 1536], P('shard')
- out_norm_gain_grad: float32 [256], P('shard')
- out_weight_grad: float32 [1536, 1024], P('shard')
- norm2_gain_grad: float32 [1024], P('shard')
- ffn_gate_grad: float32 [1024, 2816], P('shard')
- ffn_up_grad: float32 [1024, 2816], P('shard')
- ffn_down_grad: float32 [2816, 1024], P('shard')
Inputs may be any that keep to these rules, and one draw needn't show every extreme that they name: `deal`: within each replica's 2048 entries, a permutation of 0 to 2048 - 1 (a given row is numbered within its replica); each block takes exactly 32 rows from each device's given rows. `offsets`: per block, the first slots of up to 4 sequences: multiples of 64, not falling, the first 0; an entry equal to 256 means no sequence. `lengths`: each sequence's live tokens, from half of its slots to all of them, 0 exactly where there is no sequence; some sequence fills a whole block.
All inputs are finite; a program needn't handle non-finite values.
Results may differ from a plain program's by a relative error of at most 0.018.
Values may be sent and summed in bfloat16 or wider, within the bound.
A program may use at most 256 MiB of HBM per device.

v0:
```python
import functools
import jax
import jax.numpy as jnp
from jax import lax
from jax.experimental import pallas as pl
from jax.experimental.pallas import tpu as pltpu
from jax.sharding import PartitionSpec as P

f32 = jnp.float32
bf16 = jnp.bfloat16
HEADS = 6
DK = 128
DVH = 256
KEYS = 768
VALS = 1536
QKV = 2 * KEYS + VALS
LANES = 128


def two_parts(a):
    hi = a.astype(bf16)
    return hi, (a - hi.astype(f32)).astype(bf16)


def dot(a, b, ca=1, cb=0):
    return lax.dot_general(a, b, (((ca,), (cb,)), ((), ())), preferred_element_type=f32)


def dot3(a, b, ca=1, cb=0):
    ah, al = a
    bh, bl = b
    return dot(ah, bh, ca, cb) + (dot(ah, bl, ca, cb) + dot(al, bh, ca, cb))


def tri_dot(tri, cols):
    hi = cols.astype(bf16)
    rest = cols - hi.astype(f32)
    mid = rest.astype(bf16)
    lo = (rest - mid.astype(f32)).astype(bf16)
    return dot(tri, hi) + (dot(tri, mid) + dot(tri, lo))


def sigm(a):
    return 1.0 / (1.0 + jnp.exp(-a))


def softplus(a):
    return jnp.maximum(a, 0.0) + jnp.log1p(jnp.exp(-jnp.abs(a)))


def layout_cols(offs, lens, n, shape, dim):
    row = lax.broadcasted_iota(jnp.int32, shape, dim)
    begin = jnp.zeros_like(row)
    extent = jnp.zeros_like(row)
    for i in range(len(offs)):
        inside = row >= offs[i]
        begin = jnp.where(inside, offs[i], begin)
        extent = jnp.where(inside, lens[i], extent)
    return begin, row - begin, (row - begin) < extent


def conv_chunk(x, taps, pos, cols):
    total = taps[0:1, cols] * x
    for t in range(1, 4):
        total = total + taps[t : t + 1, cols] * jnp.where(pos >= t, pltpu.roll(x, t, 0), 0.0)
    return total


def lane_pick(a, lane, index):
    return jnp.sum(jnp.where(lane == index, a, 0.0), axis=1, keepdims=True)


def pair_masks(n, begin_c, begin_r):
    i = lax.broadcasted_iota(jnp.int32, (n, n), 0)
    j = lax.broadcasted_iota(jnp.int32, (n, n), 1)
    same = begin_c == begin_r
    return i, j, (i >= j) & same


def mixer_forward(n, offs, lens, lin, taps, rate, bias, gain, act, cum, cum_t, tinv, fresh, heads_out, mixed):
    begin_c, pos, live = layout_cols(offs, lens, n, (n, 1), 0)
    begin_r, _, _ = layout_cols(offs, lens, n, (1, n), 1)
    live_f = live.astype(f32)
    width = 384

    def conv_step(step, carry):
        cols = pl.ds(pl.multiple_of(step * width, width), width)
        pre = conv_chunk(lin[:, cols], taps, pos, cols)
        act[:, cols] = pre * sigm(pre)
        return carry

    lane = lax.broadcasted_iota(jnp.int32, (n, LANES), 1)
    bd = lin[:, QKV + VALS : QKV + VALS + LANES]
    beta = sigm(bd) * live_f
    decay = -jnp.exp(rate[...]) * softplus(bd + bias[...]) * live_f
    i, j, low = pair_masks(n, begin_c, begin_r)
    eye = (i == j).astype(f32)

    def convolve():
        lax.fori_loop(0, QKV // width, conv_step, 0)
        total = tri_dot((i >= j).astype(bf16), decay)
        cum[...] = total
        cum_t[...] = total.T

    def one_head(h):
        kcols = pl.ds(pl.multiple_of(h * DK, DK), DK)
        ka = act[:, pl.ds(pl.multiple_of(KEYS + h * DK, DK), DK)]
        qa = act[:, kcols]
        vcols = pl.ds(pl.multiple_of(h * DVH, DVH), DVH)
        v = act[:, pl.ds(pl.multiple_of(2 * KEYS + h * DVH, DVH), DVH)]
        q = qa * (lax.rsqrt(jnp.sum(qa * qa, axis=1, keepdims=True) + 1e-6) * DK**-0.5)
        k = ka * lax.rsqrt(jnp.sum(ka * ka, axis=1, keepdims=True) + 1e-6)
        beta_c = lane_pick(beta, lane, h)
        cum_c = lane_pick(cum[...], lane, HEADS + h)
        cum_r = cum_t[pl.ds(HEADS + h, 1), :]
        kk, qq = two_parts(k), two_parts(q)
        dec = jnp.where(low, jnp.exp(jnp.where(low, cum_c - cum_r, 0.0)), 0.0)
        system = jnp.where(i > j, beta_c * dot3(kk, kk, 1, 1) * dec, 0.0)
        inv = eye - jnp.where((i // 2) == (j // 2), system, 0.0)
        size = 2
        while size < n:
            off = jnp.where(((i // (2 * size)) == (j // (2 * size))) & ((i // size) != (j // size)), system, 0.0)
            parts = two_parts(inv)
            inv = inv - dot3(two_parts(dot3(parts, two_parts(off))), parts)
            size *= 2
        tinv[h] = inv
        u = dot3(two_parts(inv), two_parts(beta_c * v))
        fresh[:, vcols] = u
        o = dot3(two_parts(dot3(qq, kk, 1, 1) * dec), two_parts(u)) * live_f
        heads_out[:, vcols] = o
        gate = lin[:, pl.ds(pl.multiple_of(QKV + h * DVH, DVH), DVH)]
        scaled = o * lax.rsqrt(jnp.mean(o * o, axis=1, keepdims=True) + 1e-5)
        mixed[:, vcols] = (scaled * gain[...] * (gate * sigm(gate))).astype(bf16)

    return convolve, [functools.partial(one_head, h) for h in range(HEADS)]


def mixer_backward(
    n, offs, lens, lin, taps, rate, bias, gain, act, cum, cum_t, tinv, fresh, heads_out, grad_mixed,
    dact, dcols, drows, lin_grad, tap_grad, gain_grad, rate_grad, bias_grad,
):
    begin_c, pos, live = layout_cols(offs, lens, n, (n, 1), 0)
    begin_r, _, _ = layout_cols(offs, lens, n, (1, n), 1)
    live_f = live.astype(f32)
    lane = lax.broadcasted_iota(jnp.int32, (n, LANES), 1)
    bd = lin[:, QKV + VALS : QKV + VALS + LANES]
    sig_b = sigm(bd)
    beta = sig_b * live_f
    i, j, low = pair_masks(n, begin_c, begin_r)
    strict = low & (i > j)

    def clear():
        gain_grad[...] = jnp.zeros_like(gain_grad)
        dcols[...] = jnp.zeros_like(dcols)
        drows[...] = jnp.zeros_like(drows)

    def one_head(h):
        kcols = pl.ds(pl.multiple_of(h * DK, DK), DK)
        kcols2 = pl.ds(pl.multiple_of(KEYS + h * DK, DK), DK)
        vcols = pl.ds(pl.multiple_of(h * DVH, DVH), DVH)
        vcols2 = pl.ds(pl.multiple_of(2 * KEYS + h * DVH, DVH), DVH)
        gcols = pl.ds(pl.multiple_of(QKV + h * DVH, DVH), DVH)
        ka = act[:, kcols2]
        qa = act[:, kcols]
        v = act[:, vcols2]
        o = heads_out[:, vcols]
        gate = lin[:, gcols]
        dm = grad_mixed[:, vcols]
        ro = lax.rsqrt(jnp.mean(o * o, axis=1, keepdims=True) + 1e-5)
        scaled = o * ro
        sg = sigm(gate)
        si = gate * sg
        gain_grad[...] += jnp.sum(dm * scaled * si, axis=0, keepdims=True)
        lin_grad[:, gcols] = (dm * scaled * gain[...] * (sg + si * (1.0 - sg))).astype(bf16)
        ds = dm * gain[...] * si
        d_o = two_parts(ro * (ds - scaled * jnp.mean(ds * scaled, axis=1, keepdims=True)) * live_f)
        rq = lax.rsqrt(jnp.sum(qa * qa, axis=1, keepdims=True) + 1e-6)
        rk = lax.rsqrt(jnp.sum(ka * ka, axis=1, keepdims=True) + 1e-6)
        qhat = qa * rq
        k = ka * rk
        kk, qq = two_parts(k), two_parts(qhat * DK**-0.5)
        beta_c = lane_pick(beta, lane, h)
        cum_c = lane_pick(cum[...], lane, HEADS + h)
        cum_r = cum_t[pl.ds(HEADS + h, 1), :]
        dec = jnp.where(low, jnp.exp(jnp.where(low, cum_c - cum_r, 0.0)), 0.0)
        gram = dot3(kk, kk, 1, 1)
        qk = dot3(qq, kk, 1, 1)
        uu = two_parts(fresh[:, vcols])
        du = dot3(two_parts(qk * dec), d_o, 0, 0)
        dp = dot3(d_o, uu, 1, 1) * dec
        db = dot3(two_parts(tinv[h]), two_parts(du), 0, 0)
        da = jnp.where(strict, -dot3(two_parts(db), uu, 1, 1), 0.0) * dec
        x = da * gram
        dbeta = jnp.sum(x, axis=1, keepdims=True) + jnp.sum(db * v, axis=1, keepdims=True)
        e = dp * qk + x * beta_c
        dcols[...] += jnp.where(lane == h, dbeta, 0.0) + jnp.where(
            lane == HEADS + h, jnp.sum(e, axis=1, keepdims=True), 0.0
        )
        drows[pl.ds(HEADS + h, 1), :] = jnp.sum(e, axis=0, keepdims=True)
        dact[:, vcols2] = beta_c * db
        dg = two_parts(da * beta_c)
        dpp = two_parts(dp)
        dq = dot3(dpp, kk)
        dk = dot3(dpp, qq, 0, 0) + dot3(dg, kk) + dot3(dg, kk, 0, 0)
        dact[:, kcols] = (rq * DK**-0.5) * (dq - qhat * jnp.sum(dq * qhat, axis=1, keepdims=True))
        dact[:, kcols2] = rk * (dk - k * jnp.sum(dk * k, axis=1, keepdims=True))

    def rates():
        dcum = jnp.where((lane >= HEADS) & (lane < 2 * HEADS), dcols[...] - drows[...].T, 0.0)
        ddecay = tri_dot((i <= j).astype(bf16), dcum)
        z = bd + bias[...]
        speed = -jnp.exp(rate[...]) * live_f
        dz = ddecay * speed * sigm(z)
        rate_grad[...] = jnp.sum(ddecay * speed * softplus(z), axis=0, keepdims=True)
        bias_grad[...] = jnp.sum(dz, axis=0, keepdims=True)
        dbeta_lin = dcols[...] * live_f * sig_b * (1.0 - sig_b)
        both = jnp.where(lane < HEADS, dbeta_lin, jnp.where(lane < 2 * HEADS, dz, 0.0))
        lin_grad[:, QKV + VALS : QKV + VALS + LANES] = both.astype(bf16)

    width = 384

    def conv_step(step, carry):
        cols = pl.ds(pl.multiple_of(step * width, width), width)
        x = lin[:, cols]
        pre = conv_chunk(x, taps, pos, cols)
        sg = sigm(pre)
        dc = dact[:, cols] * (sg + pre * sg * (1.0 - sg))
        dx = taps[0:1, cols] * dc
        tap_grad[0:1, cols] = jnp.sum(dc * x, axis=0, keepdims=True)
        for t in range(1, 4):
            masked = jnp.where(pos >= t, dc, 0.0)
            dx = dx + taps[t : t + 1, cols] * pltpu.roll(masked, n - t, 0)
            tap_grad[t : t + 1, cols] = jnp.sum(masked * pltpu.roll(x, t, 0), axis=0, keepdims=True)
        lin_grad[:, cols] = dx.astype(bf16)
        return carry

    def convolve(first, last):
        return lambda: lax.fori_loop(first, last, conv_step, 0)

    heads = [functools.partial(one_head, h) for h in range(HEADS)]
    total = QKV // width
    return clear, heads, rates, [convolve(0, total // 2), convolve(total // 2, total)]


MESH = pl.DeviceIdType.MESH


class Place:
    def __init__(self, n_shard, n_rep):
        self.n, self.reps = n_shard, n_rep
        self.ys = n_shard // 4
        self.r = lax.axis_index("rep")
        self.s = lax.axis_index("shard")
        self.c = self.s % 2
        self.x = (self.s // 2) % 2
        self.y = self.s // 4
        half = n_rep // 2
        low = self.r < half
        self.depth = jnp.where(low, self.r, n_rep - 1 - self.r)
        self.inner = jnp.where(low, self.r + 1, self.r - 1)
        self.outer = jnp.where(low, self.r - 1, self.r + 1)
        self.middle = self.depth == half - 1
        self.deep = self.depth > 0
        self.half = self.depth % 2

    def partner(self):
        return (self.r + 1 - 2 * (self.r % 2), self.s)

    def shard_id(self, y, x, c):
        return (self.r, (y * 2 + x) * 2 + c)

    def core_peer(self):
        return self.shard_id(self.y, self.x, 1 - self.c)

    def x_peer(self):
        return self.shard_id(self.y, 1 - self.x, self.c)

    def y_of(self, step):
        return (self.y + step) % self.ys

    def y_peer(self, step):
        return self.shard_id(self.y_of(step), self.x, self.c)


def remote(src, dst, send, recv, device):
    return pltpu.make_async_remote_copy(
        src_ref=src, dst_ref=dst, send_sem=send, recv_sem=recv, device_id=device, device_id_type=MESH
    )


def greet(place, with_rep):
    barrier = pltpu.get_barrier_semaphore()
    n = place.n
    for step in range(1, n):
        pl.semaphore_signal(
            barrier, inc=1, device_id=(place.r, (place.s + step) % n), device_id_type=MESH
        )
    if not with_rep:
        pl.semaphore_wait(barrier, n - 1)
        return
    for step in range(1, place.reps):
        pl.semaphore_signal(
            barrier, inc=1, device_id=((place.r + step) % place.reps, place.s), device_id_type=MESH
        )
    pl.semaphore_wait(barrier, n - 1 + place.reps - 1)


def add_into(dst, idx, *others):
    total = dst[idx].astype(f32)
    for ref, at in others:
        total = total + ref[at].astype(f32)
    dst[idx] = total.astype(dst.dtype)


RING = 10
ZRING = 12


def halved(rows):
    return (rows // 2) // 16 * 16


class Ring:
    def __init__(self, n, rows, cols, twins=1):
        self.n, self.rows, self.cols, self.twins = n, rows, cols, twins
        self.ys = n // 4
        self.count = 0

    def scratch(self):
        k, ys, cols = RING, self.ys, self.cols
        sems = pltpu.SemaphoreType.DMA
        per = 3 + 2 * (ys - 1)
        half = self.rows - halved(self.rows)
        return [
            pltpu.VMEM((k, ys, 2, 2, self.rows, cols), bf16),
            pltpu.VMEM((k, ys, 2, self.rows, cols), bf16),
            pltpu.VMEM((k, ys, half, cols), bf16),
            pltpu.VMEM((k, ys - 1, 2, half, cols), bf16),
            pltpu.VMEM((k, ys - 1, half, cols), bf16),
            pltpu.VMEM((k, half, cols), bf16),
            pltpu.VMEM((4, ZRING, self.twins, self.rows, cols), bf16),
            sems((k, per)),
            sems((k, per)),
            sems((ZRING, 6 + self.twins)),
        ]

    def bind(self, refs):
        (self.own, self.r0, self.r1a, self.r1b, self.r2a, self.r2b, self.z, self.send, self.recv, self.zsem) = refs


class Piece:
    def __init__(self, ring, place, rows, cols, out, out_cols):
        self.ring, self.p, self.rows = ring, place, rows
        self.twin = len(out_cols) == 2
        self.side = pl.ds(0, len(out_cols))
        self.slot, self.zslot = ring.count % RING, ring.count % ZRING
        ring.count += 1
        self.w = pl.ds(0, cols)
        self.ra = halved(rows)
        self.rb = rows - self.ra
        self.all_rows = pl.ds(0, rows)
        self.outs = [out.at[:, pl.ds(at, cols)] for at in out_cols]

    def own_view(self):
        return self.ring.own.at[self.slot, :, :, :, self.all_rows, self.w]

    def store_rows(self, value):
        ring = self.ring
        shaped = value.reshape(ring.ys, 2, 2, rinself.rows, value.shape[-1])
        ring.own[self.slot, :, :, :, self.all_rows, self.w] = shaped

    def send_core(self):
        g, p, k = self.ring, self.p, self.slot
        self.c0 = remote(
            g.own.at[k, :, :, 1 - p.c, self.all_rows, self.w], g.r0.at[k, :, :, self.all_rows, self.w],
            g.send.at[k, 0], g.recv.at[k, 0], p.core_peer(),
        )
        self.c0.start()

    def after_core(self):
        g, p, k, w = self.ring, self.p, self.slot, self.w
        rows = self.all_rows
        self.c0.wait()

        def step(q, carry):
            yy, xx = q // 2, q % 2
            add_into(g.own, (k, yy, xx, p.c, rows, w), (g.r0, (k, yy, xx, rows, w)))
            return carry

        lax.fori_loop(0, g.ys * 2, step, 0)
        top, low = pl.ds(0, self.ra), pl.ds(self.ra, self.rb)
        first, second = pl.ds(0, self.ra), pl.ds(0, self.rb)
        self.c1 = [
            remote(
                g.own.at[k, :, 1 - p.x, p.c, top, w], g.r1a.at[k, :, first, w],
                g.send.at[k, 1], g.recv.at[k, 1], p.x_peer(),
            )
        ]
        for d in range(1, g.ys):
            self.c1.append(
                remote(
                    g.own.at[k, p.y_of(d), :, p.c, low, w], g.r1b.at[k, d - 1, :, second, w],
                    g.send.at[k, 1 + d], g.recv.at[k, 1 + d], p.y_peer(d),
                )
            )
        for c in self.c1:
            c.start()

    def after_first(self):
        g, p, k, w = self.ring, self.p, self.slot, self.w
        top, low = pl.ds(0, self.ra), pl.ds(self.ra, self.rb)
        first, second = pl.ds(0, self.ra), pl.ds(0, self.rb)
        for c in self.c1:
            c.wait()
        for yy in range(g.ys):
            add_into(g.own, (k, yy, p.x, p.c, top, w), (g.r1a, (k, yy, first, w)))
        for xx in range(2):
            add_into(
                g.own, (k, p.y, xx, p.c, low, w),
                *[(g.r1b, (k, d, xx, second, w)) for d in range(g.ys - 1)],
            )
        self.c2 = [
            remote(
                g.own.at[k, p.y, 1 - p.x, p.c, low, w], g.r2b.at[k, second, w],
                g.send.at[k, 1 + g.ys], g.recv.at[k, 1 + g.ys], p.x_peer(),
            )
        ]
        for d in range(1, g.ys):
            self.c2.append(
                remote(
                    g.own.at[k, p.y_of(d), p.x, p.c, top, w], g.r2a.at[k, d - 1, first, w],
                    g.send.at[k, 1 + g.ys + d], g.recv.at[k, 1 + g.ys + d], p.y_peer(d),
                )
            )
        for c in self.c2:
            c.start()

    def after_second(self):
        g, p, k, w = self.ring, self.p, self.slot, self.w
        zk = self.zslot
        for c in self.c2:
            c.wait()
        top, low = pl.ds(0, self.ra), pl.ds(self.ra, self.rb)
        total = g.own[k, p.y, p.x, p.c, top, w].astype(f32)
        for d in range(g.ys - 1):
            total = total + g.r2a[k, d, 0 : self.ra, w].astype(f32)
        side = p.half if self.twin else 0
        g.z[0, zk, side, top, w] = total.astype(bf16)
        total = g.own[k, p.y, p.x, p.c, low, w].astype(f32) + g.r2b[k, 0 : self.rb, w].astype(f32)
        g.z[0, zk, side, low, w] = total.astype(bf16)
        if self.twin:
            g.z[0, zk, 1 - side, self.all_rows, w] = jnp.zeros((self.rows, w.size), bf16)
        z = lambda i: g.z.at[i, zk, self.side, self.all_rows, w]
        target = lambda r: (r, p.s)
        sem = g.zsem
        self.up = remote(z(0), z(1), sem.at[zk, 0], sem.at[zk, 1], target(p.inner))
        self.meet = remote(z(0), z(2), sem.at[zk, 2], sem.at[zk, 3], target(p.inner))
        self.down = remote(z(3), z(2), sem.at[zk, 4], sem.at[zk, 3], target(p.outer))
        self.home = [
            pltpu.make_async_copy(g.z.at[3, zk, i, self.all_rows, w], out, sem.at[zk, 6 + i])
            for i, out in enumerate(self.outs)
        ]

        @pl.when(p.depth == 0)
        def _():
            self.send_inward()

    def send_inward(self):
        p = self.p

        @pl.when(p.middle)
        def _():
            self.meet.start()

        @pl.when(jnp.logical_not(p.middle))
        def _():
            self.up.start()

    def after_up(self):
        g, p, zk, w = self.ring, self.p, self.zslot, self.w

        @pl.when(p.deep)
        def _():
            self.up.wait_recv()
            for i in range(len(self.outs)):
                add_into(g.z, (0, zk, i, self.all_rows, w), (g.z, (1, zk, i, self.all_rows, w)))
            self.send_inward()

    def finish(self, middle):
        g, p, zk, w = self.ring, self.p, self.zslot, self.w
        rows = self.all_rows

        @pl.when(p.middle if middle else jnp.logical_not(p.middle))
        def _():
            self.meet.wait_recv()
            for i in range(len(self.outs)):
                if middle:
                    both = g.z[0, zk, i, rows, w].astype(f32) + g.z[2, zk, i, rows, w].astype(f32)
                    g.z[3, zk, i, rows, w] = both.astype(bf16)
                else:
                    g.z[3, zk, i, rows, w] = g.z[2, zk, i, rows, w]

            @pl.when(p.deep)
            def _():
                self.down.start()

            for c in self.home:
                c.start()

    def close(self):
        p = self.p

        @pl.when(p.middle)
        def _():
            self.meet.wait_send()

        @pl.when(jnp.logical_not(p.middle))
        def _():
            self.up.wait_send()

        @pl.when(p.deep)
        def _():
            self.down.wait_send()

        for c in self.home:
            c.wait()


def pump(pieces, index):
    stages = [
        (2, lambda q: q.after_core()),
        (18, lambda q: q.close()),
        (17, lambda q: q.finish(False)),
        (14, lambda q: q.finish(True)),
        (11, lambda q: q.after_up()),
        (8, lambda q: q.after_second()),
        (5, lambda q: q.after_first()),
    ]
    for lag, act in stages:
        if 0 <= index - lag < len(pieces):
            act(pieces[index - lag])


class Small:
    def __init__(self, n, reps, rows, cols):
        self.n, self.ys, self.reps = n, n // 4, reps
        self.sizes = (2, 2, self.ys, reps)
        self.rows, self.cols = rows, cols

    def scratch(self):
        total = sum(self.sizes)
        return [
            pltpu.VMEM((total, self.rows, self.cols), f32),
            pltpu.SemaphoreType.DMA((total,)),
            pltpu.SemaphoreType.DMA((total,)),
        ]

    def bind(self, refs):
        self.buf, self.send, self.recv = refs

    def begin(self, place, axis, value):
        base = sum(self.sizes[:axis])
        size = self.sizes[axis]
        p = place
        mine = (p.c, p.x, p.y, p.r)[axis]
        slot = self.buf.at[base + mine]
        slot[...] = value
        self.copies = []
        for d in range(1, size):
            at = (mine + d) % size
            device = (
                p.shard_id(p.y, p.x, at), p.shard_id(p.y, at, p.c), p.shard_id(at, p.x, p.c), (at, p.s),
            )[axis]
            self.copies.append(remote(slot, slot, self.send.at[base + d], self.recv.at[base + d], device))
        for c in self.copies:
            c.start()

    def end(self, axis):
        base = sum(self.sizes[:axis])
        for c in self.copies:
            c.wait()
        total = self.buf[base]
        for d in range(1, self.sizes[axis]):
            total = total + self.buf[base + d]
        return total


class Flow:
    @staticmethod
    def count(ys, pair):
        return 5 + 12 * (ys - 1) if pair else 3 + 6 * (ys - 1)

    def __init__(self, place, src, src_at, cols, dst, dst_at, pair, send, recv, base, mine):
        self.p, self.rows, self.pair = place, src.shape[0], pair
        self.src_ref, self.src_at, self.dst, self.dst_at, self.width = src, src_at, dst, dst_at, cols
        self.send, self.recv, self.base, self.used = send, recv, base, 0
        self.ra = halved(self.rows)
        self.part = (place.r % 2) if pair else None
        whole = self.src_ref.at[:, self.columns(src_at, None)]
        self.mine = pltpu.make_async_copy(whole, self.region(place.y, place.x, place.c), mine)
        self.whole = whole
        self.all = []

    def columns(self, at, part):
        if part is None:
            return pl.ds(at if isinstance(at, int) else pl.multiple_of(at, LANES), self.width)
        half = self.width // 2
        return pl.ds(pl.multiple_of(at + part * half, LANES), half)

    def region(self, y, x, c, half=None, part=None):
        start = ((y * 2 + x) * 2 + c) * self.rows
        size = self.rows
        if half == 0:
            size = self.ra
        elif half == 1:
            start, size = start + self.ra, self.rows - self.ra
        return self.dst.at[pl.ds(pl.multiple_of(start, 16), size), self.columns(self.dst_at, part)]

    def copy(self, dst, device, src=None):
        at = self.base + self.used
        self.used += 1
        c = remote(dst if src is None else src, dst, self.send.at[at], self.recv.at[at], device)
        c.start()
        self.all.append(c)
        return c

    def begin(self):
        p = self.p
        own = self.region(p.y, p.x, p.c, None, self.part)
        src = self.src_ref.at[:, self.columns(self.src_at, self.part)]
        self.mine.start()
        self.from_x = self.copy(own, p.x_peer(), src)
        self.from_y = [self.copy(own, p.y_peer(d), src) for d in range(1, p.ys)]
        self.from_core = [self.copy(self.region(p.y, p.x, p.c), p.core_peer(), self.whole)]
        self.from_z, self.z_regions = [], []

    def share(self, *where):
        p = self.p
        if self.pair:
            self.from_z.append(self.copy(self.region(*where, self.part), (p.r + 1 - 2 * (p.r % 2), p.s)))
            self.z_regions.append(where)
        self.from_core.append(self.copy(self.region(*where, self.part), p.core_peer()))

    def forward(self):
        p = self.p
        steps = range(1, p.ys)
        self.from_x.wait_recv()
        self.diag = [self.copy(self.region(p.y, 1 - p.x, p.c, 0, self.part), p.y_peer(d)) for d in steps]
        self.share(p.y, 1 - p.x, p.c, None)
        for d in steps:
            self.from_y[d - 1].wait_recv()
            back = p.y_of(p.ys - d)
            self.diag.append(self.copy(self.region(back, p.x, p.c, 1, self.part), p.x_peer()))
            self.share(back, p.x, p.c, None)

    def relay(self):
        p = self.p
        for i, c in enumerate(self.diag):
            c.wait_recv()
            half, d = divmod(i, p.ys - 1)
            self.share(p.y_of(p.ys - d - 1), 1 - p.x, p.c, half)

    def swap(self):
        for c, where in zip(self.from_z, self.z_regions):
            c.wait_recv()
            self.from_core.append(self.copy(self.region(*where, 1 - self.part), self.p.core_peer()))

    def done(self):
        for c in self.from_core:
            c.wait_recv()
        self.mine.wait()

    def close(self):
        for c in self.all:
            c.wait_send()


FTILE = 256
FF_TILE = 512


def cuts(total, step):
    return [(at, min(step, total - at)) for at in range(0, total, step)]


def decay_lanes(words):
    lane = lax.broadcasted_iota(jnp.int32, (1, LANES), 1)
    total = jnp.zeros((1, LANES), f32)
    for h in range(HEADS):
        total = jnp.where(lane == HEADS + h, words[h], total)
    return total


def one_hot_rows(values, count):
    return lax.broadcasted_iota(jnp.int32, (count, values.shape[1]), 0) == values


class Store:
    def __init__(self, sem):
        self.sem, self.all = sem, []

    def put(self, src, dst):
        c = pltpu.make_async_copy(src, dst, self.sem.at[len(self.all)])
        c.start()
        self.all.append(c)

    def wait(self):
        for c in self.all:
            c.wait()


FORWARD_SAVED = (
    ("xin", lambda n, d, f: ((n, d), bf16)),
    ("dy", lambda n, d, f: ((2 * n, d), bf16)),
    ("normed_t", lambda n, d, f: ((d, n), bf16)),
    ("lin", lambda n, d, f: ((n, QKV + VALS + LANES), f32)),
    ("act", lambda n, d, f: ((n, QKV), f32)),
    ("cum", lambda n, d, f: ((n, LANES), f32)),
    ("cum_t", lambda n, d, f: ((LANES, n), f32)),
    ("tinv", lambda n, d, f: ((HEADS, n, n), f32)),
    ("fresh", lambda n, d, f: ((n, VALS), f32)),
    ("heads", lambda n, d, f: ((n, VALS), f32)),
    ("mixed_t", lambda n, d, f: ((VALS, n), bf16)),
    ("middle", lambda n, d, f: ((n, d), f32)),
    ("normed_mid_t", lambda n, d, f: ((d, 2 * n), bf16)),
    ("hidden_t", lambda n, d, f: ((f // 2, 2 * n), bf16)),
    ("grads_gu", lambda n, d, f: ((2 * n, f), bf16)),
    ("pick", lambda n, d, f: ((n, n), bf16)),
    ("place", lambda n, d, f: ((n, n), bf16)),
    ("params", lambda n, d, f: ((16, d), f32)),
    ("taps", lambda n, d, f: ((4, QKV), f32)),
)


def transposed(a):
    return a.T.astype(bf16)


def forward_kernel(n_shard, reps, *refs):
    take = iter(refs)
    get = lambda k: [next(take) for _ in range(k)]
    offs, lens, rates_in, bias_in, tokens, cot, deal, small_in = get(8)
    wq, wk, wv, wt, wb, wo, wg, wu, wd = get(9)
    gp, go, gg, gu, gd = get(5)
    outs = dict(zip([name for name, _ in FORWARD_SAVED], get(len(FORWARD_SAVED))))
    kept = dict(zip([name for name, _ in FORWARD_SAVED], get(len(FORWARD_SAVED))))
    (dealt, dsend, drecv, smalls, ssend, srecv, sent, come, tsend, trecv, wbuf, wobuf, wdbuf, load_sem, fsend, frecv,
     mine_sem, out_sem, normed, mixed, normed_mid) = get(21)
    shards, shard_sem, zsend, zrecv = get(9), *get(3)
    rate, bias = get(2)
    rate[...], bias[...] = decay_lanes(rates_in), decay_lanes(bias_in)
    own_loads = []
    for k, (w, v) in enumerate(zip((wq, wk, wv, wt, wb, wo, wd, wg, wu), shards)):
        own_loads.append(pltpu.make_async_copy(w, v, shard_sem.at[k]))
        own_loads[-1].start()
    wq, wk, wv, wt, wb, wo, wd, wg, wu = shards
    rows, width = tokens.shape
    per = rows // n_shard
    place = Place(n_shard, reps)
    p = place
    greet(place, True)
    offsets = [offs[i] for i in range(offs.shape[0])]
    lengths = [lens[i] for i in range(lens.shape[0])]
    store = Store(out_sem)

    dealt[p.s] = jnp.broadcast_to(deal[...], (8, rows))
    smalls[p.s] = small_in[...]
    first = []
    for d in range(1, n_shard):
        to = (p.r, (p.s + d) % n_shard)
        first.append(remote(dealt.at[p.s], dealt.at[p.s], dsend.at[d], drecv.at[d], to))
        first[-1].start()
    for d in range(1, n_shard):
        to = (p.r, (p.s + d) % n_shard)
        first.append(remote(smalls.at[p.s], smalls.at[p.s], ssend.at[d], srecv.at[d], to))
        first[-1].start()

    made = []

    def flow(src, at, cols, dst, dst_at, pair):
        k = len(made)
        base = sum(Flow.count(p.ys, f.pair) for f in made)
        made.append(Flow(place, src, at, cols, dst, dst_at, pair, fsend, frecv, base, mine_sem.at[k]))
        return made[-1]

    ff = wg.shape[1]
    half = ff // 2
    ff_cuts = cuts(half, FF_TILE)
    stages = [
        [flow(wq, 0, KEYS, gp, 0, True), flow(wk, 0, KEYS, gp, KEYS, True), flow(wb, 0, LANES, gp, QKV + VALS, False)],
        [flow(wv, 0, VALS, gp, 2 * KEYS, True)],
        [flow(wt, 0, VALS, gp, QKV, False)],
        [flow(wo, 0, width, go, 0, True)],
        [flow(wd, 0, width // 2, gd, 0, False)],
        [flow(wd, width // 2, width // 2, gd, width // 2, False)],
    ]
    for at, cols in ff_cuts:
        stages.append([flow(wg, p.half * half + at, cols, gg, at, False), flow(wu, p.half * half + at, cols, gu, at, False)])
    last = len(stages) - 1

    events = []
    for k in range(len(stages) + 5):
        for lag, act in ((0, "begin"), (2, "forward"), (3, "relay"), (4, "swap"), (5, "done")):
            if 0 <= k - lag < len(stages):
                events.append((act, k - lag))
    owned = set()

    def poll(count=1):
        for _ in range(count):
            if events:
                act, k = events.pop(0)
                for f in stages[k]:
                    if act == "begin" and id(f.src_ref) not in owned:
                        owned.add(id(f.src_ref))
                        own_loads[[id(v) for v in shards].index(id(f.src_ref))].wait()
                    getattr(f, act)()

    def until(act, k):
        while (act, k) in events:
            poll()

    until("begin", 1)

    loads = {}

    def load(name, src, dst):
        loads[name] = pltpu.make_async_copy(src, dst, load_sem.at[len(loads)])
        loads[name].start()

    for c in first[: n_shard - 1]:
        c.wait_recv()
    i = lax.broadcasted_iota(jnp.int32, (rows, rows), 0)
    j = lax.broadcasted_iota(jnp.int32, (rows, rows), 1)
    upper = (i <= j).astype(bf16)
    everyone = dealt[:, 0, :]
    to_me = (everyone // rows) == p.s
    rank = dot(to_me.astype(f32).astype(bf16), upper).astype(jnp.int32) - 1
    rank = jnp.where(to_me, rank, -1)
    for b in range(n_shard):
        picked = one_hot_rows(rank[b : b + 1, :], per).astype(f32).astype(bf16)
        which = one_hot_rows(everyone[b : b + 1, :] % rows, rows).astype(f32).astype(bf16)
        kept["pick"][b * per : (b + 1) * per, :] = dot(picked, which, 1, 1).astype(bf16)
    pick = kept["pick"][...]
    exchange = []
    for a, src in enumerate((tokens, cot)):
        for at in range(0, width, 256):
            sent[a, :, at : at + 256] = dot(pick, src[:, at : at + 256]).astype(bf16)
        for d in range(1, n_shard):
            t = (p.s + d) % n_shard
            exchange.append(
                remote(
                    sent.at[a, pl.ds(pl.multiple_of(t * per, 16), per)],
                    come.at[a, pl.ds(pl.multiple_of(p.s * per, 16), per)],
                    tsend.at[a, d], trecv.at[a, d], (p.r, t),
                )
            )
            exchange[-1].start()
        here = pl.ds(pl.multiple_of(p.s * per, 16), per)
        come[a, here, :] = sent[a, here, :]
    mine = deal[0:1, :]
    source = mine // rows
    from_each = one_hot_rows(source, n_shard)
    cum = dot(from_each.astype(f32).astype(bf16), upper)
    slot = jnp.sum(jnp.where(from_each, cum, 0.0), axis=0, keepdims=True).astype(jnp.int32) - 1 + source * per
    kept["place"][...] = one_hot_rows(slot, rows).astype(f32).astype(bf16)
    store.put(kept["pick"], outs["pick"])
    store.put(kept["place"], outs["place"])

    for c in first[n_shard - 1 :]:
        c.wait_recv()
    total = smalls[0].astype(f32)
    for t in range(1, n_shard):
        total = total + smalls[t].astype(f32)
    kept["params"][...] = total
    for t in range(4):
        for g in range(QKV // width):
            row = t * (QKV // width) + g
            kept["taps"][t : t + 1, g * width : (g + 1) * width] = total[row : row + 1, :]
    gain1, gain2 = kept["params"].at[12:13, :], kept["params"].at[13:14, :]
    gain_o = kept["params"].at[14:15, 0:DVH]
    store.put(kept["params"], outs["params"])
    store.put(kept["taps"], outs["taps"])

    def unpack(a, name):
        for c in exchange[a * (n_shard - 1) : (a + 1) * (n_shard - 1)]:
            c.wait_recv()
        for at in range(0, width, 256):
            kept[name][0:rows, at : at + 256] = dot(kept["place"][...], come[a, :, at : at + 256], 0, 0).astype(bf16)
    unpack(0, "xin")
    store.put(kept["xin"], outs["xin"])

    def swap_rows(ref, k):
        c = remote(ref.at[pl.ds(0, rows)], ref.at[pl.ds(rows, rows)], zsend.at[k], zrecv.at[k], p.partner())
        c.start()
        return c

    x = kept["xin"][...].astype(f32)
    norm = x * lax.rsqrt(jnp.mean(x * x, axis=1, keepdims=True) + 1e-5) * gain1[...]
    normed[...] = norm.astype(bf16)
    kept["normed_t"][...] = transposed(norm)
    store.put(kept["normed_t"], outs["normed_t"])

    def project(at, cols, tile):
        def step(k, carry):
            here = pl.ds(pl.multiple_of(at + k * tile, 128), tile)
            kept["lin"][:, here] = dot(normed[...], wbuf[:, here])
            return carry

        lax.fori_loop(0, cols // tile, step, 0)

    def fetch(name, at, cols):
        here = pl.ds(at, cols)
        load(name, gp.at[:, here], wbuf.at[:, here])

    until("done", 0)
    fetch("qk", 0, 2 * KEYS)
    fetch("bd", QKV + VALS, LANES)
    until("done", 1)
    fetch("v", 2 * KEYS, VALS)
    loads["qk"].wait()
    loads["bd"].wait()
    project(0, 2 * KEYS, 256)
    project(QKV + VALS, LANES, LANES)
    poll(1)
    loads["v"].wait()
    project(2 * KEYS, VALS, 256)
    until("done", 2)
    fetch("gate", QKV, VALS)
    convolve, heads = mixer_forward(
        rows, offsets, lengths, kept["lin"], kept["taps"], rate, bias, gain_o, kept["act"], kept["cum"],
        kept["cum_t"], kept["tinv"], kept["fresh"], kept["heads"], mixed,
    )
    convolve()
    unpack(1, "dy")
    dy_swap = swap_rows(kept["dy"], 0)
    loads["gate"].wait()
    project(QKV, VALS, 256)
    store.put(kept["lin"], outs["lin"])
    for h in range(0, HEADS, 2):
        heads[h]()
        heads[h + 1]()
        poll(6)
    until("done", 3)
    load("out", go, wobuf)
    for name in ("act", "cum", "cum_t", "tinv", "fresh", "heads"):
        store.put(kept[name], outs[name])
    loads["out"].wait()

    def out_step(k, carry):
        here = pl.ds(pl.multiple_of(k * 256, 256), 256)
        kept["middle"][:, here] = kept["xin"][:, here].astype(f32) + dot(mixed[...], wobuf[:, here])
        return carry

    lax.fori_loop(0, width // 256, out_step, 0)
    store.put(kept["middle"], outs["middle"])
    m = kept["middle"][...]
    norm = m * lax.rsqrt(jnp.mean(m * m, axis=1, keepdims=True) + 1e-5) * gain2[...]
    normed_mid[0:rows, :] = norm.astype(bf16)
    mid_swap = swap_rows(normed_mid, 1)
    kept["normed_mid_t"][:, 0:rows] = transposed(norm)
    kept["mixed_t"][...] = transposed(mixed[...].astype(f32))
    store.put(kept["mixed_t"], outs["mixed_t"])
    until("done", 5)
    load("down", gd.at[pl.ds(pl.multiple_of(p.half * half, LANES), half)], wdbuf)

    def ffn(at, cols):
        def step(k, carry):
            some = pl.ds(pl.multiple_of(k * rows, rows), rows)
            here, there = slice(at, at + cols), slice(half + at, half + at + cols)
            grad = dot(kept["dy"][some, :], wdbuf[here, :], 1, 1)
            gate = dot(normed_mid[some, :], wbuf[:, here])
            up = dot(normed_mid[some, :], wbuf[:, there])
            sg = sigm(gate)
            silu = gate * sg
            hid = silu * up
            kept["hidden_t"][here, some] = transposed(hid)
            kept["grads_gu"][some, here] = (grad * up * (sg + silu * (1.0 - sg))).astype(bf16)
            kept["grads_gu"][some, there] = (grad * silu).astype(bf16)
            return carry

        lax.fori_loop(0, 2, step, 0)

    for i, (at, cols) in enumerate(ff_cuts):
        until("done", last - len(ff_cuts) + 1 + i)
        load(("g", i), gg.at[:, pl.ds(at, cols)], wbuf.at[:, pl.ds(at, cols)])
        load(("u", i), gu.at[:, pl.ds(at, cols)], wbuf.at[:, pl.ds(half + at, cols)])
        if i == 0:
            loads["down"].wait()
            dy_swap.wait()
            mid_swap.wait()
            store.put(kept["dy"], outs["dy"])
            kept["normed_mid_t"][:, rows : 2 * rows] = transposed(normed_mid[rows : 2 * rows, :].astype(f32))
            store.put(kept["normed_mid_t"], outs["normed_mid_t"])
        poll(2)
        loads[("g", i)].wait()
        loads[("u", i)].wait()
        ffn(at, cols)
    for name in ("hidden_t", "grads_gu"):
        store.put(kept[name], outs[name])
    for c in first + exchange:
        c.wait_send()
    for f in made:
        f.close()
    store.wait()


def forward_call(n_shard, reps, offs, lens, tokens, cot, deal, small_in, rate, bias, weights):
    anywhere = pl.BlockSpec(memory_space=pl.ANY)
    held = pl.BlockSpec(memory_space=pltpu.VMEM)
    words = pl.BlockSpec(memory_space=pltpu.SMEM)
    rows, width = tokens.shape
    ff = weights[6].shape[1]
    sd = jax.ShapeDtypeStruct
    wide = QKV + VALS + LANES
    vals_rows, ff_rows = weights[5].shape[0] * n_shard, weights[8].shape[0] * n_shard
    gathered = [
        sd((width, wide), bf16), sd((vals_rows, width), bf16), sd((width, ff // 2), bf16), sd((width, ff // 2), bf16),
        sd((ff_rows, width), bf16),
    ]
    shapes = [fn(rows, width, ff) for _, fn in FORWARD_SAVED]
    sems = pltpu.SemaphoreType.DMA
    flows = 8 + 2 * len(cuts(ff // 2, FF_TILE))
    count = flows * Flow.count(n_shard // 4, True)
    scratch = [pltpu.VMEM(s, d) for s, d in shapes] + [
        pltpu.VMEM((n_shard, 8, rows), jnp.int32), sems((n_shard,)), sems((n_shard,)),
        pltpu.VMEM((n_shard, 16, width), bf16), sems((n_shard,)), sems((n_shard,)),
        pltpu.VMEM((2, rows, width), bf16), pltpu.VMEM((2, rows, width), bf16), sems((2, n_shard)), sems((2, n_shard)),
        pltpu.VMEM((width, wide), bf16), pltpu.VMEM((vals_rows, width), bf16), pltpu.VMEM((ff_rows // 2, width), bf16),
        sems((16,)), sems((count,)), sems((count,)), sems((flows,)), sems((len(shapes),)),
        pltpu.VMEM((rows, width), bf16), pltpu.VMEM((rows, VALS), bf16), pltpu.VMEM((2 * rows, width), bf16),
    ]
    scratch += [pltpu.VMEM(weights[k].shape, bf16) for k in (0, 1, 2, 3, 4, 5, 8, 6, 7)] + [sems((9,)), sems((2,)), sems((2,))]
    scratch += [pltpu.VMEM((1, LANES), f32)] * 2
    res = pl.pallas_call(
        functools.partial(forward_kernel, n_shard, reps),
        in_specs=[words] * 4 + [held] * 4 + [anywhere] * 9,
        out_specs=[anywhere] * (5 + len(shapes)),
        out_shape=gathered + [sd(s, d) for s, d in shapes],
        scratch_shapes=scratch,
        compiler_params=pltpu.CompilerParams(collective_id=1, has_side_effects=True, vmem_limit_bytes=62 << 20),
    )(offs, lens, rate, bias, tokens, cot, deal, small_in, *weights)
    return res[:5], dict(zip([name for name, _ in FORWARD_SAVED], res[5:]))


WIDE = 512
PIECE = 256


class Stream:
    def __init__(self, buf, sem, parts):
        self.buf, self.sem, self.parts, self.at = buf, sem, parts, 0
        self.copies = {}

    def start(self):
        self.issue(0)

    def issue(self, k):
        if k < len(self.parts):
            pairs = self.parts[k](self.buf.at[k % 2])
            self.copies[k] = [pltpu.make_async_copy(s, d, self.sem.at[k % 2, i]) for i, (s, d) in enumerate(pairs)]
            for c in self.copies[k]:
                c.start()

    def take(self):
        k = self.at
        self.at += 1
        self.issue(k + 1)
        for c in self.copies[k]:
            c.wait()
        return k, self.buf.at[k % 2]


BACK_KEPT = tuple(name for name, _ in FORWARD_SAVED)


def backward_kernel(n_shard, reps, rings, small, *refs):
    take = iter(refs)
    get = lambda k: [next(take) for _ in range(k)]
    offs, lens, rates_in, bias_in = get(4)
    gp, go, gg, gu, gd = get(5)
    given = dict(zip(BACK_KEPT, get(len(BACK_KEPT))))
    o_rows, o_grad, o_ffn, o_down, o_out, o_proj, o_small = get(7)
    kept = dict(zip(BACK_KEPT, get(len(BACK_KEPT))))
    (ring,) = rings
    ring.bind(get(10))
    small.bind(get(3))
    (load_sem, wbuf, wsem, nbuf, nsem, acc, middle_grad, branch, mix_grad, dcols, drows, lin_grad, tap_grad, gain_grad,
     rate_grad, bias_grad, small_v, sent, come, tsend, trecv, rows_out, out_sem, swaps, zsend, zrecv, block, rate, bias) = get(29)
    rate[...], bias[...] = decay_lanes(rates_in), decay_lanes(bias_in)
    rows, width = kept["xin"].shape
    half = gg.shape[1]
    ff = 2 * half
    per = rows // n_shard
    place = Place(n_shard, reps)
    p = place
    offsets = [offs[i] for i in range(offs.shape[0])]
    lengths = [lens[i] for i in range(lens.shape[0])]
    loads = {}
    order = (
        "normed_mid_t", "grads_gu", "middle", "dy", "params", "hidden_t", "cum", "cum_t", "tinv", "fresh", "heads",
        "act", "lin", "taps", "mixed_t", "normed_t", "xin", "pick", "place",
    )
    for k, name in enumerate(order):
        loads[name] = pltpu.make_async_copy(given[name], kept[name], load_sem.at[k])
        loads[name].start()
    have = set()

    def need(*names):
        for name in names:
            if name not in have:
                have.add(name)
                loads[name].wait()

    greet(place, True)
    pieces = []

    def tick(piece=None, fill=None):
        index = tick.index
        tick.index += 1
        pump(pieces, index)
        if piece is not None:
            pieces.append(piece())
            fill(pieces[-1])
            pieces[-1].send_core()

    tick.index = 0

    size = width // n_shard

    def wide_piece(left, right, right_at, cols, out, out_at):
        def fill(piece):
            value = dot(left[...], right[:, right_at : right_at + cols]).astype(bf16)
            ring.own[piece.slot, :, :, :, :, 0:cols] = value.reshape(ring.ys, 2, 2, size, cols)

        tick(lambda: Piece(ring, place, size, cols, out, out_at), fill)

    def block_piece(left, right, at, cols, first, count, out):
        total = left.shape[0]
        long = out.shape[0]
        held = total // long
        ys = held // 4

        def fill(piece):
            if first == 0:
                block[0:total, 0:cols] = dot(left[...], right[:, at : at + cols]).astype(bf16)
            for t in range(held):
                y = t // 4 if held == n_shard else p.half * ys + t // 4
                part = block[t * long + first : t * long + first + count, 0:cols]
                ring.own[piece.slot, y, (t // 2) % 2, t % 2, 0:count, 0:cols] = part
            if held < n_shard:
                for t in range(held):
                    y = (1 - p.half) * ys + t // 4
                    ring.own[piece.slot, y, (t // 2) % 2, t % 2, 0:count, 0:cols] = jnp.zeros((count, cols), bf16)

        tick(lambda: Piece(ring, place, count, cols, out.at[pl.ds(first, count)], (at,)), fill)

    queue = []

    def run(count=1):
        for _ in range(count):
            queue.pop(0)()

    gu_cuts = [(side, at, cols) for side in (0, 1) for at, cols in cuts(half, WIDE)]

    def gu_piece(side, at, cols):
        need("normed_mid_t", "grads_gu")
        outs = (side * ff + at, side * ff + half + at)
        wide_piece(kept["normed_mid_t"], kept["grads_gu"], side * half + at, cols, o_ffn, outs)

    def down_piece(at, first, count):
        need("hidden_t", "dy")
        block_piece(kept["hidden_t"], kept["dy"], at, PIECE, first, count, o_down)

    def out_piece(at, first, count):
        need("mixed_t")
        block_piece(kept["mixed_t"], branch, at, PIECE, first, count, o_out)

    def proj_piece(at, cols):
        need("normed_t")
        wide_piece(kept["normed_t"], lin_grad, at, cols, o_proj, (at,))

    def blocks(fn, out):
        return [
            functools.partial(fn, at, first, count) for at, _ in cuts(width, PIECE) for first, count in cuts(out.shape[0], size)
        ]

    sided = [functools.partial(gu_piece, side, at, cols) for side in (0, 1) for at, cols in cuts(half, PIECE)]
    downs = blocks(down_piece, o_down)
    while sided or downs:
        queue.extend(sided[:1] + downs[:1])
        del sided[:1], downs[:1]
    queue.extend(blocks(out_piece, o_out))
    wide = cuts(QKV + VALS, PIECE)
    late = QKV // PIECE
    for at, cols in wide[late:] + wide[:late] + [(QKV + VALS, LANES)]:
        queue.append(functools.partial(proj_piece, at, cols))

    def gu_part(k):
        side, at, cols = gu_cuts[k]
        return lambda b: [((gg, gu)[side].at[:, pl.ds(at, cols)], b.at[:, pl.ds(0, cols)])]

    gu_stream = Stream(wbuf, wsem, [gu_part(k) for k in range(len(gu_cuts))])

    def gnm(count):
        need("grads_gu")
        for _ in range(count):
            k, buf = gu_stream.take()
            side, at, cols = gu_cuts[k]
            at = side * half + at
            part = dot(kept["grads_gu"][:, at : at + cols], buf[:, 0:cols], 1, 1)
            acc[...] = part if k == 0 else acc[...] + part

    def to_partner(k):
        swaps[0] = acc[rows : 2 * rows, :].astype(bf16)
        c = remote(swaps.at[0], swaps.at[1 + k], zsend.at[k], zrecv.at[k], p.partner())
        c.start()
        return c

    def norm_back(values, gain, upstream):
        n = lax.rsqrt(jnp.mean(values * values, axis=1, keepdims=True) + 1e-5)
        u = upstream * gain
        gain_part = jnp.sum(upstream * values * n, axis=0, keepdims=True)
        return n * (u - values * (n * n) * jnp.mean(u * values, axis=1, keepdims=True)), gain_part

    def norm2():
        need("middle", "dy", "params")
        mid_swap.wait()
        upstream = acc[0:rows, :] + swaps[1].astype(f32)
        back, gain_part = norm_back(kept["middle"][...], kept["params"][13:14, :], upstream)
        small_v[13:14, :] = gain_part
        total = kept["dy"][0:rows, :].astype(f32) + back
        middle_grad[...] = total
        branch[...] = total.astype(bf16)

    def row_part(src, k):
        return lambda b: [(src.at[pl.ds(k * FTILE, FTILE), :], b)]

    out_stream = Stream(nbuf, nsem, [row_part(go, k) for k in range(VALS // FTILE)])
    down_cuts = cuts(half, FTILE)

    def down_part(at, size):
        start = pl.multiple_of(p.half * half + at, LANES)
        return lambda b: [(gd.at[pl.ds(start, size), :], b.at[pl.ds(0, size)])]

    down_stream = Stream(nbuf, nsem, [down_part(at, size) for at, size in down_cuts])

    def grad_mixed(count):
        for _ in range(count):
            k, buf = out_stream.take()
            mix_grad[:, k * FTILE : (k + 1) * FTILE] = dot(branch[...], buf[...], 1, 1)

    def result(count):
        need("hidden_t", "middle")
        for _ in range(count):
            k, buf = down_stream.take()
            at, size = down_cuts[k]
            part = dot(kept["hidden_t"][at : at + size, :], buf[0:size, :], 0, 0)
            acc[...] = part if k == 0 else acc[...] + part

    exchange = {}

    def send_home(a, value):
        need("place")
        here = pl.ds(pl.multiple_of(p.s * per, 16), per)
        for at in range(0, width, 256):
            sent[a, :, at : at + 256] = dot(kept["place"][...], value[:, at : at + 256]).astype(bf16)
        exchange[a] = []
        for d in range(1, n_shard):
            t = (p.s + d) % n_shard
            exchange[a].append(
                remote(
                    sent.at[a, pl.ds(pl.multiple_of(t * per, 16), per)], come.at[a, here],
                    tsend.at[a, d], trecv.at[a, d], (p.r, t),
                )
            )
            exchange[a][-1].start()
        come[a, here, :] = sent[a, here, :]

    stores = []

    def arrive(a, out):
        need("pick")
        for c in exchange[a]:
            c.wait()
        for at in range(0, width, 256):
            rows_out[a, :, at : at + 256] = dot(kept["pick"][...], come[a, :, at : at + 256], 0, 0).astype(bf16)
        stores.append(pltpu.make_async_copy(rows_out.at[a], out, out_sem.at[a]))
        stores[-1].start()

    def wide_part(at, cols):
        return lambda b: [(gp.at[:, pl.ds(at, cols)], b.at[:, pl.ds(0, cols)])]

    proj_cuts = [(at, WIDE) for at in range(0, QKV + VALS, WIDE)] + [(QKV + VALS, LANES)]
    proj_stream = Stream(wbuf, wsem, [wide_part(at, cols) for at, cols in proj_cuts])

    def grad_normed(count):
        for _ in range(count):
            k, buf = proj_stream.take()
            at, cols = proj_cuts[k]
            part = dot(lin_grad[:, at : at + cols], buf[:, 0:cols], 1, 1)
            acc[0:rows, :] = part if k == 0 else acc[0:rows, :] + part

    def norm1():
        need("xin")
        back, gain_part = norm_back(kept["xin"][...].astype(f32), kept["params"][12:13, :], acc[0:rows, :])
        small_v[12:13, :] = gain_part
        rows_out[1] = (middle_grad[...] + back).astype(bf16)

    def pack_small():
        small_v[14:16, :] = jnp.zeros((2, width), f32)
        for t in range(4):
            for g in range(QKV // width):
                row = t * (QKV // width) + g
                small_v[row : row + 1, :] = tap_grad[t : t + 1, g * width : (g + 1) * width]
        small_v[14:15, 0:DVH] = gain_grad[...]
        small_v[14:15, DVH : DVH + LANES] = rate_grad[...]
        small_v[14:15, DVH + LANES : DVH + 2 * LANES] = bias_grad[...]

    gu_stream.start()
    out_stream.start()
    for _ in gu_cuts:
        run()
        gnm(1)
    mid_swap = to_partner(0)
    run(6)
    need("cum", "cum_t", "tinv", "fresh", "heads", "act", "lin", "taps")
    clear, heads, rates, convs = mixer_backward(
        rows, offsets, lengths, kept["lin"], kept["taps"], rate, bias, kept["params"].at[14:15, 0:DVH], kept["act"],
        kept["cum"], kept["cum_t"], kept["tinv"], kept["fresh"], kept["heads"], mix_grad,
        kept["act"], dcols, drows, lin_grad, tap_grad, gain_grad, rate_grad, bias_grad,
    )
    clear()
    norm2()
    run()
    grad_mixed(3)
    run()
    grad_mixed(3)
    down_stream.start()
    for head in heads:
        run(2)
        head()
    for step in [rates] + convs:
        run()
        step()
    while len(queue) > len(wide) + 1:
        run()
    result(3)
    run()
    result(len(down_cuts) - 3)
    result_swap = to_partner(1)
    proj_stream.start()
    run(4)
    result_swap.wait()
    rows_out[0] = (kept["middle"][...] + acc[0:rows, :] + swaps[2].astype(f32)).astype(bf16)
    send_home(0, rows_out.at[0])
    run()
    for count in (3, 3, len(proj_cuts) - 6):
        grad_normed(count)
        run()
    norm1()
    send_home(1, rows_out.at[1])
    pack_small()
    value = small_v[...]
    for k in range(4):
        small.begin(place, k, value)
        run()
        value = small.end(k)
    arrive(0, o_rows)
    run()
    arrive(1, o_grad)
    run(len(queue))
    for _ in range(18):
        tick()
    o_small[...] = value
    for c in stores:
        c.wait()


def backward_call(n_shard, reps, offs, lens, rate, bias, gathered, saved):
    anywhere = pl.BlockSpec(memory_space=pl.ANY)
    held = pl.BlockSpec(memory_space=pltpu.VMEM)
    words = pl.BlockSpec(memory_space=pltpu.SMEM)
    rows, width = saved["xin"].shape
    ff = 2 * gathered[2].shape[1]
    sd = jax.ShapeDtypeStruct
    wide = QKV + VALS + LANES
    sems = pltpu.SemaphoreType.DMA
    rings = (Ring(n_shard, width // n_shard, PIECE, 2),)
    small = Small(n_shard, reps, 16, width)
    outs = [
        sd((rows, width), bf16), sd((rows, width), bf16), sd((width // n_shard, 2 * ff), bf16),
        sd((ff // n_shard, width), bf16), sd((VALS // n_shard, width), bf16), sd((width // n_shard, wide), bf16),
        sd((16, width), f32),
    ]
    vmem = pltpu.VMEM
    scratch = [vmem(saved[name].shape, saved[name].dtype) for name in BACK_KEPT]
    scratch += rings[0].scratch() + small.scratch()
    scratch += [
        sems((len(BACK_KEPT),)), vmem((2, width, WIDE), bf16), sems((2, 2)), vmem((2, FTILE, width), bf16), sems((2, 1)),
        vmem((2 * rows, width), f32), vmem((rows, width), f32), vmem((rows, width), bf16), vmem((rows, VALS), f32),
        vmem((rows, LANES), f32), vmem((LANES, rows), f32), vmem((rows, wide), bf16), vmem((4, QKV), f32),
        vmem((1, DVH), f32), vmem((1, LANES), f32), vmem((1, LANES), f32), vmem((16, width), f32),
        vmem((2, rows, width), bf16), vmem((2, rows, width), bf16), sems((2, n_shard)), sems((2, n_shard)),
        vmem((2, rows, width), bf16), sems((2,)), vmem((3, rows, width), bf16), sems((2,)), sems((2,)),
        vmem((max(VALS, ff // 2), PIECE), bf16), vmem((1, LANES), f32), vmem((1, LANES), f32),
    ]
    return pl.pallas_call(
        functools.partial(backward_kernel, n_shard, reps, rings, small),
        in_specs=[words] * 4 + [anywhere] * (5 + len(BACK_KEPT)),
        out_specs=[anywhere] * 6 + [held],
        out_shape=outs,
        scratch_shapes=scratch,
        compiler_params=pltpu.CompilerParams(collective_id=0, has_side_effects=True, vmem_limit_bytes=63 << 20),
    )(offs, lens, rate, bias, *gathered, *[saved[name] for name in BACK_KEPT])


def local(
    reps, tokens, cotangent, deal, offsets, lengths, norm1_gain, q_weight, k_weight, v_weight, conv_weight,
    beta_weight, decay_weight, log_rate, step_bias, out_gate_weight, out_norm_gain, out_weight, norm2_gain,
    ffn_gate, ffn_up, ffn_down,
):
    rows, width = tokens.shape
    n = lax.axis_size("shard")
    s = lax.axis_index("shard")
    pad = LANES - 2 * HEADS
    bd_weight = jnp.concatenate([beta_weight, decay_weight, jnp.zeros((beta_weight.shape[0], pad), bf16)], axis=1)
    def spread(vector):
        k, size = vector.shape
        mine = jnp.arange(n)[None, :, None] == s
        return jnp.where(mine, vector[:, None, :], jnp.zeros((), bf16)).reshape(-1, min(width, n * size))

    gain = spread(out_norm_gain[None])
    small_in = jnp.concatenate(
        [
            spread(conv_weight), spread(norm1_gain[None]), spread(norm2_gain[None]),
            jnp.pad(gain, ((0, 1), (0, width - gain.shape[1]))),
        ]
    )
    weights = (q_weight, k_weight, v_weight, out_gate_weight, bd_weight, out_weight, ffn_gate, ffn_up, ffn_down)
    deals = deal[None, :]
    gathered, saved = forward_call(
        n, reps, offsets[0], lengths[0], tokens, cotangent, deals, small_in, log_rate, step_bias, weights
    )
    home_rows, home_grad, s_ffn, s_down, s_out, s_proj, small = backward_call(
        n, reps, offsets[0], lengths[0], log_rate, step_bias, gathered, saved
    )

    def part(a, dim=0):
        size = a.shape[dim] // n
        return lax.dynamic_slice_in_dim(a, s * size, size, dim)

    at = QKV + VALS
    ff = ffn_gate.shape[1]
    proj = [(0, 0, KEYS), (0, KEYS, KEYS), (0, 2 * KEYS, VALS), (0, QKV, VALS), (0, at, LANES)]
    rest = [(1, 0, ff), (1, ff, ff), (2, 0, width), (3, 0, width)]
    g_q, g_k, g_v, g_t, g_bd, g_gate, g_up, g_down, g_out = widen([s_proj, s_ffn, s_down, s_out], proj + rest)
    return (
        home_rows, home_grad, part(small[12]), g_q, g_k, g_v, part(small[:12].reshape(4, QKV), 1), g_bd[:, :HEADS],
        g_bd[:, HEADS : 2 * HEADS], small[14, DVH + HEADS : DVH + 2 * HEADS],
        small[14, DVH + LANES + HEADS : DVH + LANES + 2 * HEADS], g_t, part(small[14, :DVH]), g_out, part(small[13]),
        g_gate, g_up, g_down,
    )


def widen(sources, cut):
    k, total = len(sources), len(cut)

    def kernel(*refs):
        ins, outs = refs[:k], refs[k : k + total]
        narrow, wide = refs[k + total : 2 * k + total], refs[2 * k + total : 2 * (k + total)]
        come, go = refs[2 * (k + total) :]
        for i in range(k):
            pltpu.make_async_copy(ins[i], narrow[i], come.at[i]).start()
        ready = set()
        for j, (i, at, cols) in enumerate(cut):
            if i not in ready:
                ready.add(i)
                pltpu.make_async_copy(ins[i], narrow[i], come.at[i]).wait()
            wide[j][...] = narrow[i][:, at : at + cols].astype(f32)
            pltpu.make_async_copy(wide[j], outs[j], go.at[j]).start()
        for j in range(total):
            pltpu.make_async_copy(wide[j], outs[j], go.at[j]).wait()

    anywhere = pl.BlockSpec(memory_space=pl.ANY)
    shapes = [(sources[i].shape[0], cols) for i, _, cols in cut]
    return pl.pallas_call(
        kernel,
        in_specs=[anywhere] * k,
        out_specs=[anywhere] * total,
        out_shape=[jax.ShapeDtypeStruct(shape, f32) for shape in shapes],
        scratch_shapes=[pltpu.VMEM(a.shape, bf16) for a in sources]
        + [pltpu.VMEM(shape, f32) for shape in shapes]
        + [pltpu.SemaphoreType.DMA((k,)), pltpu.SemaphoreType.DMA((total,))],
        compiler_params=pltpu.CompilerParams(vmem_limit_bytes=62 << 20),
    )(*sources)


def solution(mesh):
    rows2, shard0 = P(("rep", "shard"), None), P("shard", None)
    vec = P("shard")
    in_specs = (
        rows2, rows2, P(("rep", "shard")), rows2, rows2, vec, shard0, shard0, shard0, P(None, "shard"),
        shard0, shard0, P(), P(), shard0, vec, shard0, vec, shard0, shard0, shard0,
    )
    out_specs = (
        rows2, rows2, vec, shard0, shard0, shard0, P(None, "shard"), shard0, shard0, P(), P(), shard0,
        vec, shard0, vec, shard0, shard0, shard0,
    )
    body = functools.partial(local, mesh.shape["rep"])
    return jax.shard_map(body, mesh=mesh, in_specs=in_specs, out_specs=out_specs, check_vma=False)
```

profile of v0, /device:TPU:0, one launch (start us, length us, event | category | flops | bytes accessed | tf_op | source)
XLA Modules:
  0.0 339.2 jit_solution(7101117264717945685)
XLA Ops:
  0.7 0.7 broadcast_bitcast_fusion.1
  1.4 0.8 broadcast_select_fusion
  2.3 0.1 broadcast_in_dim.101
  2.3 0.1 broadcast_in_dim.102
  2.4 0.7 broadcast_in_dim.103
  3.1 0.1 broadcast_in_dim.104
  3.2 0.6 fusion.1.refs_7_
  3.8 0.8 copy.39
  4.6 0.8 copy.40
  5.4 0.1 pad.7.clone
  5.5 0.7 maximum_maximum_fusion.refs_12_
  6.2 151.4 %shard_map.340 = (bf16[1024,4736]{1,0:T(8,128)(2,1)}, bf16[1536,1024]{1,0:T(8,128)(2,1)}, bf16[1024,1408]{1,0:T(8,128)(2,1)}, bf16[1024,1408]{1,0:T(8,128)(2,1)}...) custom-call(s32[4]{0:T(128)} %bitcast.33, ...), custom_call_target="tpu_custom_call" | custom-call | tf_op jit(solution)/shard_map/pallas_call | solution.py:1034
  157.7 170.0 %shard_map.341 = (bf16[256,1024]{1,0:T(8,128)(2,1)}, bf16[256,1024]{1,0:T(8,128)(2,1)}, bf16[128,5632]{1,0:T(8,128)(2,1)}, bf16[352,1024]{1,0:T(8,128)(2,1)}, bf...) custom-call(s32[4]{0:T(128)} %bitcast.34, s32[4]{0:T(128)} %bitcast.36, f32[6]{0:T(128)} %refs_2_.3, ...), custom_call_target="tpu_custom_call" | custom-call | tf_op jit(solution)/shard_map/pallas_call | solution.py:1407
  327.7 4.5 %shard_map.342 = (f32[128,768]{1,0:T(8,128)}, f32[128,768]{1,0:T(8,128)}, f32[128,1536]{1,0:T(8,128)}, f32[128,1536]{1,0:T(8,128)}, f32[128,128]{1,0:T(8,128)}, ...) custom-call(bf16[128,4736]{1,0:T(8,128)(2,1)} %get-tuple-element.85.refs_0_, ...), custom_call_target="tpu_custom_call" | custom-call | tf_op jit(solution)/shard_map/pallas_call | solution.py:1486
  332.2 1.0 fusion.6
  333.2 0.7 copy.41
  333.9 0.7 copy.42
  334.6 0.6 constant_dynamic-slice_fusion.2
  335.2 0.5 fusion.2
  335.7 0.5 fusion.4
  336.3 0.6 fusion.3
  336.8 0.6 slice_bitcast_fusion
  337.4 0.8 copy.52
  338.2 0.8 copy.53
  (15 shorter events, 0.2 us)
Async XLA Ops:
  327.6 6.9 %copy-start.2 = (f32[16,1024]{1,0:T(8,128)S(1)}, f32[16,1024]{1,0:T(8,128)}, u32[]{:S(2)}) copy-start(f32[16,1024]{1,0:T(8,128)} %get-tuple-element.84) | copy-start | bytes 196612
  327.7 9.8 %copy-start.1 = (bf16[256,1024]{1,0:T(8,128)(2,1)S(1)}, bf16[256,1024]{1,0:T(8,128)(2,1)}, u32[]{:S(2)}) copy-start(bf16[256,1024]{1,0:T(8,128)(2,1)} %get-tuple-element.144) | copy-start | bytes 1572868
  332.2 6.0 %copy-start = (bf16[256,1024]{1,0:T(8,128)(2,1)S(1)}, bf16[256,1024]{1,0:T(8,128)(2,1)}, u32[]{:S(2)}) copy-start(bf16[256,1024]{1,0:T(8,128)(2,1)} %get-tuple-element.145) | copy-start | bytes 1572868
where the time goes:
time: 344 us; the launch traced here: 339 us
  Pallas kernels  326 us (95%)
  local copies, waits for them, and re-layouts  10.2 us (3%)
    pallas_call x1, Pallas kernels, backward_call(): pl.pallas_call(functools.partial(backward_kernel, n_shard, reps, rings, s...  170 us
    pallas_call x1, Pallas kernels, forward_call(): pl.pallas_call(functools.partial(forward_kernel, n_shard, reps), in_specs...  151 us

commit v1 on v0

--- a/solution.py
+++ b/solution.py
@@ -897,8 +897,6 @@
     x = kept["xin"][...].astype(f32)
     norm = x * lax.rsqrt(jnp.mean(x * x, axis=1, keepdims=True) + 1e-5) * gain1[...]
     normed[...] = norm.astype(bf16)
-    kept["normed_t"][...] = transposed(norm)
-    store.put(kept["normed_t"], outs["normed_t"])
 
     def project(at, cols, tile):
         def step(k, carry):
@@ -963,38 +961,37 @@
     until("done", 5)
     load("down", gd.at[pl.ds(pl.multiple_of(p.half * half, LANES), half)], wdbuf)
 
-    def ffn(at, cols):
-        def step(k, carry):
-            some = pl.ds(pl.multiple_of(k * rows, rows), rows)
-            here, there = slice(at, at + cols), slice(half + at, half + at + cols)
-            grad = dot(kept["dy"][some, :], wdbuf[here, :], 1, 1)
-            gate = dot(normed_mid[some, :], wbuf[:, here])
-            up = dot(normed_mid[some, :], wbuf[:, there])
-            sg = sigm(gate)
-            silu = gate * sg
-            hid = silu * up
-            kept["hidden_t"][here, some] = transposed(hid)
-            kept["grads_gu"][some, here] = (grad * up * (sg + silu * (1.0 - sg))).astype(bf16)
-            kept["grads_gu"][some, there] = (grad * silu).astype(bf16)
-            return carry
-
-        lax.fori_loop(0, 2, step, 0)
-
+    def ffn(k, at, cols):
+        some = slice(k * rows, (k + 1) * rows)
+        here, there = slice(at, at + cols), slice(half + at, half + at + cols)
+        grad = dot(kept["dy"][some, :], wdbuf[here, :], 1, 1)
+        gate = dot(normed_mid[some, :], wbuf[:, here])
+        up = dot(normed_mid[some, :], wbuf[:, there])
+        sg = sigm(gate)
+        silu = gate * sg
+        hid = silu * up
+        kept["hidden_t"][here, some] = transposed(hid)
+        kept["grads_gu"][some, here] = (grad * up * (sg + silu * (1.0 - sg))).astype(bf16)
+        kept["grads_gu"][some, there] = (grad * silu).astype(bf16)
+
+    loads["down"].wait()
     for i, (at, cols) in enumerate(ff_cuts):
         until("done", last - len(ff_cuts) + 1 + i)
         load(("g", i), gg.at[:, pl.ds(at, cols)], wbuf.at[:, pl.ds(at, cols)])
         load(("u", i), gu.at[:, pl.ds(at, cols)], wbuf.at[:, pl.ds(half + at, cols)])
-        if i == 0:
-            loads["down"].wait()
-            dy_swap.wait()
-            mid_swap.wait()
-            store.put(kept["dy"], outs["dy"])
-            kept["normed_mid_t"][:, rows : 2 * rows] = transposed(normed_mid[rows : 2 * rows, :].astype(f32))
-            store.put(kept["normed_mid_t"], outs["normed_mid_t"])
         poll(2)
         loads[("g", i)].wait()
         loads[("u", i)].wait()
-        ffn(at, cols)
+        ffn(0, at, cols)
+    kept["normed_t"][...] = transposed(normed[...].astype(f32))
+    store.put(kept["normed_t"], outs["normed_t"])
+    dy_swap.wait()
+    mid_swap.wait()
+    store.put(kept["dy"], outs["dy"])
+    for at, cols in ff_cuts:
+        ffn(1, at, cols)
+    kept["normed_mid_t"][:, rows : 2 * rows] = transposed(normed_mid[rows : 2 * rows, :].astype(f32))
+    store.put(kept["normed_mid_t"], outs["normed_mid_t"])
     for name in ("hidden_t", "grads_gu"):
         store.put(kept[name], outs[name])
     for c in first + exchange:

time: 344 us -> 338 us (0.983)
  Pallas kernels: 326 us -> 321 us
    pallas_call x1, Pallas kernels: 151 us -> 145 us  [forward_call(): pl.pallas_call(functools.partial(forward_kernel, n_shard, reps), in_specs...]
where the time goes in v1:
time: 338 us; the launch traced here: 334 us
  Pallas kernels  321 us (95%)
  local copies, waits for them, and re-layouts  10.2 us (3%)
    pallas_call x1, Pallas kernels, backward_call(): pl.pallas_call(functools.partial(backward_kernel, n_shard, reps, rings, s...  171 us
    pallas_call x1, Pallas kernels, forward_call(): pl.pallas_call(functools.partial(forward_kernel, n_shard, reps), in_specs...  145 us

profile of v1, /device:TPU:0, one launch (start us, length us, event | category | flops | bytes accessed | tf_op | source)
XLA Modules:
  0.0 333.8 jit_solution(7945705907641237164)
XLA Ops:
  0.7 0.1 broadcast_bitcast_fusion
  0.7 0.7 broadcast_bitcast_fusion.1
  1.4 0.8 broadcast_select_fusion
  2.3 0.1 broadcast_in_dim.102
  2.4 0.7 broadcast_in_dim.103
  3.1 0.1 broadcast_in_dim.104
  3.2 0.6 fusion.1.refs_7_
  3.8 0.8 copy.39
  4.6 0.8 copy.40
  5.4 0.1 pad.7.clone
  5.5 0.7 maximum_maximum_fusion.refs_12_
  6.2 145.1 %shard_map.340 = (bf16[1024,4736]{1,0:T(8,128)(2,1)}, bf16[1536,1024]{1,0:T(8,128)(2,1)}, bf16[1024,1408]{1,0:T(8,128)(2,1)}, bf16[1024,1408]{1,0:T(8,128)(2,1)}...) custom-call(s32[4]{0:T(128)} %bitcast.33, ...), custom_call_target="tpu_custom_call" | custom-call | tf_op jit(solution)/shard_map/pallas_call | solution.py:1031
  151.3 170.9 %shard_map.341 = (bf16[256,1024]{1,0:T(8,128)(2,1)}, bf16[256,1024]{1,0:T(8,128)(2,1)}, bf16[128,5632]{1,0:T(8,128)(2,1)}, bf16[352,1024]{1,0:T(8,128)(2,1)}, bf...) custom-call(s32[4]{0:T(128)} %bitcast.34, s32[4]{0:T(128)} %bitcast.36, f32[6]{0:T(128)} %refs_2_.3, ...), custom_call_target="tpu_custom_call" | custom-call | tf_op jit(solution)/shard_map/pallas_call | solution.py:1404
  322.2 4.5 %shard_map.342 = (f32[128,768]{1,0:T(8,128)}, f32[128,768]{1,0:T(8,128)}, f32[128,1536]{1,0:T(8,128)}, f32[128,1536]{1,0:T(8,128)}, f32[128,128]{1,0:T(8,128)}, ...) custom-call(bf16[128,4736]{1,0:T(8,128)(2,1)} %get-tuple-element.85.refs_0_, ...), custom_call_target="tpu_custom_call" | custom-call | tf_op jit(solution)/shard_map/pallas_call | solution.py:1483
  326.8 1.0 fusion.6
  327.8 0.7 copy.41
  328.5 0.7 copy.42
  329.2 0.6 constant_dynamic-slice_fusion.2
  329.8 0.5 fusion.2
  330.3 0.5 fusion.4
  330.8 0.6 fusion.3
  331.4 0.6 slice_bitcast_fusion
  332.0 0.8 copy.52
  332.8 0.8 copy.53
  (15 shorter events, 0.2 us)
Async XLA Ops:
  322.2 6.9 %copy-start.2 = (f32[16,1024]{1,0:T(8,128)S(1)}, f32[16,1024]{1,0:T(8,128)}, u32[]{:S(2)}) copy-start(f32[16,1024]{1,0:T(8,128)} %get-tuple-element.84) | copy-start | bytes 196612
  322.2 9.8 %copy-start.1 = (bf16[256,1024]{1,0:T(8,128)(2,1)S(1)}, bf16[256,1024]{1,0:T(8,128)(2,1)}, u32[]{:S(2)}) copy-start(bf16[256,1024]{1,0:T(8,128)(2,1)} %get-tuple-element.144) | copy-start | bytes 1572868
  326.8 6.0 %copy-start = (bf16[256,1024]{1,0:T(8,128)(2,1)S(1)}, bf16[256,1024]{1,0:T(8,128)(2,1)}, u32[]{:S(2)}) copy-start(bf16[256,1024]{1,0:T(8,128)(2,1)} %get-tuple-element.145) | copy-start | bytes 1572868
